TPU v7x, 32 devices: a whole 2x2x4 slice. The times are simulated.
32 devices in a mesh: col: 4 (over y, x), row: 8 (over z, core).
Axes of the slice: x: 2, y: 2, z: 4, core: 2. Of those that a mesh axis runs over, the one named last changes fastest.
Arguments:
- corner_top_left: bfloat16 [400, 800], P('col', 'row'), may hold values from -0.625 to 0.625
- corner_top_right: bfloat16 [400, 800], P('col', 'row'), may hold values from -0.625 to 0.625
- corner_bottom_left: bfloat16 [400, 800], P('col', 'row'), may hold values from -0.625 to 0.625
- edge_top: bfloat16 [400, 20000], P('col', 'row'), may hold values from -6 to 6
- edge_right: bfloat16 [400, 20000], P('col', 'row'), may hold values from -6 to 6
- edge_bottom: bfloat16 [400, 20000], P('col', 'row'), may hold values from -6 to 6
- edge_left: bfloat16 [400, 20000], P('col', 'row'), may hold values from -6 to 6
- tensors: bfloat16 [8, 625, 625], replicated, may hold values from -0.25 to 0.25
- pattern: int32 [4, 8], P('col', 'row'), may hold values from 0 to 7, as said below
- sketch_below: float32 [100, 100], replicated, may hold values from -0.4375 to 0.4375
- sketch_above: float32 [100, 100], replicated, may hold values from -0.4375 to 0.4375
- sketch_right: float32 [100, 100], replicated, may hold values from -0.4375 to 0.4375
- sketch_left: float32 [100, 100], replicated, may hold values from -0.4375 to 0.4375
Outputs:
- left_corner_top: bfloat16 [400, 800], P('col', 'row')
- left_edge: bfloat16 [400, 20000], P('col', 'row')
- left_corner_bottom: bfloat16 [400, 800], P('col', 'row')
- top_corner_left: bfloat16 [400, 800], P('col', 'row')
- top_edge: bfloat16 [400, 20000], P('col', 'row')
- top_corner_right: bfloat16 [400, 800], P('col', 'row')
Inputs may be any that keep to these rules, and one draw needn't show every extreme that they name: `pattern`: each of the 8 tensors sits at exactly 4 sites.
All inputs are finite; a program needn't handle non-finite values.
Results may differ from a plain program's by a relative error of at most 0.039.
Values may be sent and summed in bfloat16 or wider, within the bound.
No kernel may reach another device: no remote copies, remote signals or barrier semaphores. Data moves between devices by JAX's collectives and lax.ppermute only.
A program may use at most 192 MiB of HBM per device.

v0:
```python
import jax
import jax.numpy as jnp
from jax import lax
from jax.sharding import PartitionSpec as P


def from_behind(value, axis, steps):
    count = lax.axis_size(axis)
    pairs = [(source, (source + steps) % count) for source in range(count)]
    return lax.ppermute(value, axis, pairs)


def rms_scale(values):
    scale = jnp.sqrt(jnp.mean(values * values) + 1e-06)
    return (values / scale).astype(jnp.bfloat16)


def orthonormal(sketched):
    gram_matrix = jnp.dot(sketched.T, sketched, precision=lax.Precision.HIGHEST)
    factor = jnp.linalg.cholesky(gram_matrix)
    return jax.scipy.linalg.solve_triangular(factor, sketched.T, lower=True).T


def sketch_with(half_field, sketch):
    return jnp.dot(half_field, sketch, precision=lax.Precision.HIGHEST)


def corner_edge(corner, edge_field, layout):
    bond_dim = corner.shape[0]
    site_dim = edge_field.shape[1] // bond_dim
    joined = jnp.einsum(
        layout,
        corner,
        edge_field.reshape(bond_dim, site_dim, bond_dim),
        preferred_element_type=jnp.float32,
    )
    return joined.reshape(bond_dim * site_dim, bond_dim)


def pad_minor(values, width):
    extra = width - values.shape[-1]
    return jnp.pad(values, [(0, 0)] * (values.ndim - 1) + [(0, extra)])


def absorb(frame_in, edge_field, arranged, frame_out):
    bond_dim = edge_field.shape[0]
    site_dim = edge_field.shape[1] // bond_dim
    padded = (bond_dim + 127) // 128 * 128
    block_in = pad_minor(
        frame_in.astype(jnp.bfloat16).reshape(bond_dim, site_dim, bond_dim), padded
    )
    block_in = block_in.reshape(bond_dim, site_dim * padded)
    edge_three = pad_minor(edge_field.reshape(bond_dim, site_dim, bond_dim), padded)
    pieces = []
    for index in range(site_dim):
        pieces.append(
            lax.dot_general(
                block_in,
                edge_three[:, index, :],
                (((0,), (0,)), ((), ())),
                preferred_element_type=jnp.float32,
            )
        )
    mixed_rows = (
        jnp.stack(pieces).astype(jnp.bfloat16).reshape(site_dim * site_dim, padded * padded)
    )
    pushed = lax.dot_general(
        arranged, mixed_rows, (((0,), (0,)), ((), ())), preferred_element_type=jnp.float32
    )
    pushed = pushed.astype(jnp.bfloat16).reshape(site_dim, site_dim * padded, padded)
    block_out = frame_out.astype(jnp.bfloat16).reshape(bond_dim, site_dim, bond_dim)
    block_out = jnp.pad(block_out, ((0, padded - bond_dim), (0, 0), (0, 0)))
    total = jnp.zeros((site_dim * padded, bond_dim), jnp.float32)
    for index in range(site_dim):
        total = total + jnp.dot(
            pushed[index], block_out[:, index, :], preferred_element_type=jnp.float32
        )
    result = total.reshape(site_dim, padded, bond_dim)[:, :bond_dim, :].transpose(1, 0, 2)
    return result.reshape(bond_dim, site_dim * bond_dim)


def body(
    corner_top_left,
    corner_top_right,
    corner_bottom_left,
    edge_top,
    edge_right,
    edge_bottom,
    edge_left,
    tensors,
    pattern,
    sketch_below,
    sketch_above,
    sketch_right,
    sketch_left,
):
    tensor = lax.dynamic_index_in_dim(tensors, pattern[0, 0], 0, keepdims=False)
    site_dim = edge_top.shape[1] // edge_top.shape[0]
    square = site_dim * site_dim
    tensor_left = (
        tensor.reshape(site_dim, site_dim, square).transpose(1, 0, 2).reshape(square, square)
    )
    tensor_top = (
        tensor.reshape(square, site_dim, site_dim).transpose(0, 2, 1).reshape(square, square)
    )
    upper_half = corner_edge(corner_top_left, edge_top, "dr,rkq->dkq")
    lower_half = corner_edge(corner_bottom_left, edge_bottom, "ur,rkq->ukq")
    lower_sketch = sketch_with(lower_half, sketch_below)
    upper_sketch = sketch_with(upper_half, sketch_above)
    from_below = from_behind(upper_sketch.astype(jnp.bfloat16), "row", -1).astype(
        upper_sketch.dtype
    )
    frame_below = orthonormal(lower_sketch + from_below)
    frame_above = from_behind(frame_below.astype(jnp.bfloat16), "row", 1).astype(frame_below.dtype)
    corner_new = rms_scale(jnp.dot(frame_above.T, upper_half, precision=lax.Precision.HIGHEST))
    bottom_new = rms_scale(jnp.dot(frame_below.T, lower_half, precision=lax.Precision.HIGHEST))
    edge_new = rms_scale(absorb(frame_above, edge_left, tensor_left, frame_below))
    side_half = corner_edge(corner_top_right, edge_right, "lu,ukd->lkd")
    side_sketch = sketch_with(side_half, sketch_right)
    head_next = corner_edge(corner_new, edge_new, "ur,ukw->rkw")
    frame_right = orthonormal(side_sketch + sketch_with(head_next, sketch_left))
    left_corner, left_edge_new, left_bottom = from_behind(
        (corner_new, edge_new, bottom_new), "col", 1
    )
    head_half = corner_edge(left_corner, left_edge_new, "ur,ukw->rkw")
    frame_left = from_behind(frame_right.astype(jnp.bfloat16), "col", 1).astype(frame_right.dtype)
    top_corner = rms_scale(jnp.dot(head_half.T, frame_left, precision=lax.Precision.HIGHEST))
    right_corner = rms_scale(jnp.dot(frame_right.T, side_half, precision=lax.Precision.HIGHEST))
    top_new = rms_scale(absorb(frame_left, edge_top, tensor_top, frame_right))
    moved_corner, moved_edge, moved_right = from_behind(
        (top_corner, top_new, right_corner), "row", 1
    )
    return (left_corner, left_edge_new, left_bottom, moved_corner, moved_edge, moved_right)


def solution(mesh):
    in_specs = (
        P("col", "row"),
        P("col", "row"),
        P("col", "row"),
        P("col", "row"),
        P("col", "row"),
        P("col", "row"),
        P("col", "row"),
        P(),
        P("col", "row"),
        P(),
        P(),
        P(),
        P(),
    )
    out_specs = (
        P("col", "row"),
        P("col", "row"),
        P("col", "row"),
        P("col", "row"),
        P("col", "row"),
        P("col", "row"),
    )
    return jax.shard_map(body, mesh=mesh, in_specs=in_specs, out_specs=out_specs, check_vma=False)
```

profile of v0, /device:TPU:0, one launch (start us, length us, event | category | flops | bytes accessed | tf_op | source)
XLA Modules:
  0.0 608.4 jit_solution(885393007652953663)
XLA Ops:
  5.8 2.2 convolution_convert_fusion.52
  8.0 4.5 collective-permute-start
  12.5 2.5 reshape.245
  16.9 2.7 reshape.219
  20.2 8.2 %fusion.328 = (bf16[625,625]{1,0:T(8,128)(2,1)S(1)}, bf16[1,625,625]{2,0,1:T(2,128)(2,1)}) fusion(bf16[8,625,625]{2,0,1:T(8,128)(2,1)} %param.23, s32[]{:T(128)S(6)} %select_n.7), kind=kLoop, calls=%fused_computation.506 | loop fusion | bytes 2343754 | tf_op jit(solution)/shard_map/jit(dynamic_index_in_dim)/dynamic_slice | solution.py:97
  29.8 2.5 copy.164
  32.2 2.3 reshape.223
  35.2 3.5 reshape.248
  40.6 2.4 reshape.232
  43.0 3.7 copy.231
  48.1 2.5 copy.232
  50.5 2.8 reshape.235
  53.4 2.8 fusion.333
  56.2 2.4 fusion.334
  58.6 2.3 fusion.105
  61.1 9.1 %cholesky.44 = f32[100,100]{1,0:T(8,128)S(1)} custom-call(f32[100,100]{1,0:T(8,128)S(1)} %fusion.118), custom_call_target="Cholesky" | custom-call | tf_op jit(solution)/shard_map/jit(cholesky)/cholesky | solution.py:20
  71.6 7.7 %custom-call.6 = f32[1,100,100]{1,2,0:T(8,128)S(1)} custom-call(f32[1,100,100]{2,1,0:T(8,128)S(1)} %fusion.113), custom_call_target="InvertDiagBlocksLowerTriangular" | custom-call | tf_op jit(solution)/shard_map/jit(_solve_triangular)/triangular_solve | solution.py:21
  79.3 2.4 fusion.102
  83.5 2.2 copy.192
  88.1 2.2 pad_slice_fusion.25
  90.4 1.7 copy.193
  95.2 1.6 copy.196
  103.0 1.6 copy.201
  106.1 1.6 copy.203
  107.7 1.6 copy.204
  119.8 3.5 multiply_reduce_fusion.4
  126.0 2.2 copy.165
  163.9 31.1 %convert_element_type.97 = bf16[625,16384]{1,0:T(8,128)(2,1)} reshape(bf16[25,3200,128]{2,1,0:T(8,128)(2,1)} %fusion.49) | data formatting | bytes 40960000 | tf_op jit(solution)/shard_map/convert_element_type | solution.py:65
  195.0 22.2 %convolution_convert_fusion.1 = bf16[625,16384]{1,0:T(8,128)(2,1)} fusion(bf16[625,625]{1,0:T(8,128)(2,1)S(1)} %copy-done.93, bf16[625,16384]{1,0:T(8,128)(2,1)} %convert_element_type.97), kind=kOutput, calls=%fused_computation.1 | convolution fusion | flops 12810240000 | bytes 41741248 | tf_op jit(solution)/shard_map/dot_general | solution.py:67
  217.2 6.5 %fusion.332 = (bf16[25,16384]{1,0:T(8,128)(2,1)}, bf16[25,16384]{1,0:T(8,128)(2,1)}, bf16[25,16384]{1,0:T(8,128)(2,1)}, bf16[25,16384]{1,0:T(8,128)(2,1)}, bf16[...) fusion(bf16[625,16384]{1,0:T(8,128)(2,1)} %convolution_convert_fusion.1), kind=kLoop, calls=%fused_computation.510 | loop fusion | bytes 9830400 | tf_op jit(solution)/shard_map/slice | solution.py:76
  223.7 15.6 %fusion.331 = (bf16[25,16384]{1,0:T(8,128)(2,1)}, bf16[25,16384]{1,0:T(8,128)(2,1)}, bf16[25,16384]{1,0:T(8,128)(2,1)}, bf16[25,16384]{1,0:T(8,128)(2,1)}, bf16[...) fusion(bf16[625,16384]{1,0:T(8,128)(2,1)} %convolution_convert_, ...), kind=kLoop, calls=%fused_computation.509 | loop fusion | bytes 31129600 | tf_op jit(solution)/shard_map/slice | solution.py:76
  239.3 2.4 multiply_reduce_fusion.5
  244.6 2.6 squeeze.481
  305.8 1.7 convolution_add_fusion.24
  307.5 1.8 copy.296
  315.2 2.7 convolution_add_fusion.48
  319.3 9.1 %cholesky.55 = f32[100,100]{1,0:T(8,128)S(1)} custom-call(f32[100,100]{1,0:T(8,128)S(1)} %fusion.116), custom_call_target="Cholesky" | custom-call | tf_op jit(solution)/shard_map/jit(cholesky)/cholesky | solution.py:20
  329.8 7.7 %custom-call.7 = f32[1,100,100]{1,2,0:T(8,128)S(1)} custom-call(f32[1,100,100]{2,1,0:T(8,128)S(1)} %fusion.114), custom_call_target="InvertDiagBlocksLowerTriangular" | custom-call | tf_op jit(solution)/shard_map/jit(_solve_triangular)/triangular_solve | solution.py:21
  340.8 2.2 copy.259
  345.3 2.1 pad_slice_fusion
  347.4 2.8 reshape.246
  382.0 1.9 multiply_reduce_fusion.2
  421.5 31.3 %convert_element_type.106 = bf16[625,16384]{1,0:T(8,128)(2,1)} reshape(bf16[25,3200,128]{2,1,0:T(8,128)(2,1)} %fusion.99) | data formatting | bytes 40960000 | tf_op jit(solution)/shard_map/convert_element_type | solution.py:65
  452.8 27.0 %convolution_convert_fusion = bf16[625,16384]{1,0:T(8,128)(2,1)} fusion(bf16[625,625]{0,1:T(8,128)(2,1)S(1)} %copy-done.92, bf16[625,16384]{1,0:T(8,128)(2,1)} %convert_element_type.106), kind=kOutput, calls=%fused_computation | convolution fusion | flops 12810240000 | bytes 41741248 | tf_op jit(solution)/shard_map/dot_general | solution.py:67
  479.8 15.8 %fusion.329 = (bf16[25,16384]{1,0:T(8,128)(2,1)S(1)}, bf16[25,16384]{1,0:T(8,128)(2,1)}, bf16[25,16384]{1,0:T(8,128)(2,1)}, bf16[25,16384]{1,0:T(8,128)(2,1)}, b...) fusion(bf16[625,16384]{1,0:T(8,128)(2,1)} %convolution_convert_, ...), kind=kLoop, calls=%fused_computation.507 | loop fusion | bytes 31129600 | tf_op jit(solution)/shard_map/slice | solution.py:76
  495.6 6.5 %fusion.330 = (bf16[25,16384]{1,0:T(8,128)(2,1)}, bf16[25,16384]{1,0:T(8,128)(2,1)}, bf16[25,16384]{1,0:T(8,128)(2,1)}, bf16[25,16384]{1,0:T(8,128)(2,1)}, bf16[...) fusion(bf16[625,16384]{1,0:T(8,128)(2,1)} %convolution_convert_fusion), kind=kLoop, calls=%fused_computation.508 | loop fusion | bytes 9830400 | tf_op jit(solution)/shard_map/slice | solution.py:76
  502.0 3.5 reshape.247
  508.2 2.3 squeeze.556
  511.8 2.5 squeeze.560
  515.6 2.3 squeeze.564
  519.2 2.3 squeeze.568
  522.8 2.3 squeeze.572
  526.5 2.3 squeeze.576
  530.1 2.3 squeeze.580
  533.8 2.3 squeeze.584
  537.4 2.3 squeeze.588
  540.9 2.3 squeeze.592
  544.6 2.3 squeeze.596
  548.2 2.7 squeeze.600
  580.4 1.7 convolution_add_fusion
  586.4 2.5 copy.306
  590.1 2.9 multiply_reduce_fusion.3
  593.8 7.1 %collective-permute-done.6 = bf16[100,100]{1,0:T(8,128)(2,1)S(1)} collective-permute-done((bf16[100,100]{1,0:T(8,128)(2,1)S(1)}, bf16[100,100]{1,0:T(8,128)(2,1)S(1)}, u32[]{:S(2)}, u32[]{:S(2)}) %collective-permute-start.6) | collective-permute-done | bytes 20032 | tf_op jit(solution)/shard_map/ppermute | solution.py:10
  602.2 1.9 copy.374
  (574 shorter events, 276.2 us)
Async XLA Ops:
  0.6 5.1 copy-start
  0.6 1.6 copy-start.155
  5.8 6.7 %copy-start.95 = (bf16[100,2500]{1,0:T(8,128)(2,1)S(1)}, bf16[100,2500]{1,0:T(8,128)(2,1)}, u32[]{:S(2)}) copy-start(bf16[100,2500]{1,0:T(8,128)(2,1)} %param.21) | copy-start | bytes 1500004
  5.8 9.2 %copy-start.156 = (bf16[100,100]{1,0:T(8,128)(2,1)S(1)}, bf16[100,100]{1,0:T(8,128)(2,1)}, u32[]{:S(2)}) copy-start(bf16[100,100]{1,0:T(8,128)(2,1)} %param.18) | copy-start | bytes 60004
  8.0 50.6 %collective-permute-start = (bf16[2500,100]{0,1:T(8,128)(2,1)}, bf16[2500,100]{0,1:T(8,128)(2,1)}, u32[]{:S(2)}, u32[]{:S(2)}) collective-permute-start(bf16[2500,100]{0,1:T(8,128)(2,1)} %convolution_convert_fusion.52), channel_id=1, source_target_pairs={{0,7},{1,0},{2,1},{3,2},{4,3},{5,4},{6,5},{7,6},{8,15},{9,8},{10,9... | collective-permute-start | bytes 1500008 | tf_op jit(solution)/shard_map/ppermute | solution.py:10
  32.2 2.3 copy-start.94
  34.9 3.8 copy-start.157
  50.5 2.8 copy-start.152
  53.4 2.8 copy-start.2
  53.4 2.8 copy-start.153
  56.2 2.4 copy-start.4
  83.5 42.5 %collective-permute-start.1 = (bf16[2500,100]{0,1:T(8,128)(2,1)}, bf16[2500,100]{0,1:T(8,128)(2,1)}, u32[]{:S(2)}, u32[]{:S(2)}) collective-permute-start(bf16[2500,100]{0,1:T(8,128)(2,1)} %convert_bitcast_fusion.1), channel_id=1, source_target_pairs={{0,1},{1,2},{2,3},{3,4},{4,5},{5,6},{6,7},{7,0},{8,9},{9,10},{10,1... | collective-permute-start | bytes 1500008 | tf_op jit(solution)/shard_map/ppermute | solution.py:10
  90.3 22.1 %copy-start.105 = (bf16[128,1,100]{2,1,0:T(2,128)(2,1)S(1)}, bf16[128,1,100]{2,1,0:T(2,128)(2,1)}, u32[]{:S(2)}) copy-start(bf16[128,1,100]{2,1,0:T(2,128)(2,1)} %get-tuple-element.105) | copy-start | bytes 76804
  90.3 22.8 %copy-start.104 = (bf16[128,1,100]{2,1,0:T(2,128)(2,1)S(1)}, bf16[128,1,100]{2,1,0:T(2,128)(2,1)}, u32[]{:S(2)}) copy-start(bf16[128,1,100]{2,1,0:T(2,128)(2,1)} %get-tuple-element.106) | copy-start | bytes 76804
  90.3 23.5 %copy-start.103 = (bf16[128,1,100]{2,1,0:T(2,128)(2,1)S(1)}, bf16[128,1,100]{2,1,0:T(2,128)(2,1)}, u32[]{:S(2)}) copy-start(bf16[128,1,100]{2,1,0:T(2,128)(2,1)} %get-tuple-element.107) | copy-start | bytes 76804
  90.3 24.3 %copy-start.102 = (bf16[128,1,100]{2,1,0:T(2,128)(2,1)S(1)}, bf16[128,1,100]{2,1,0:T(2,128)(2,1)}, u32[]{:S(2)}) copy-start(bf16[128,1,100]{2,1,0:T(2,128)(2,1)} %get-tuple-element.108) | copy-start | bytes 76804
  90.3 25.0 %copy-start.101 = (bf16[128,1,100]{2,1,0:T(2,128)(2,1)S(1)}, bf16[128,1,100]{2,1,0:T(2,128)(2,1)}, u32[]{:S(2)}) copy-start(bf16[128,1,100]{2,1,0:T(2,128)(2,1)} %get-tuple-element.109) | copy-start | bytes 76804
  90.3 25.7 %copy-start.99 = (bf16[128,1,100]{2,1,0:T(2,128)(2,1)S(1)}, bf16[128,1,100]{2,1,0:T(2,128)(2,1)}, u32[]{:S(2)}) copy-start(bf16[128,1,100]{2,1,0:T(2,128)(2,1)} %get-tuple-element.111) | copy-start | bytes 76804
  90.3 26.4 %copy-start.98 = (bf16[128,1,100]{2,1,0:T(2,128)(2,1)S(1)}, bf16[128,1,100]{2,1,0:T(2,128)(2,1)}, u32[]{:S(2)}) copy-start(bf16[128,1,100]{2,1,0:T(2,128)(2,1)} %get-tuple-element.112) | copy-start | bytes 76804
  90.4 27.1 %copy-start.97 = (bf16[128,1,100]{2,1,0:T(2,128)(2,1)S(1)}, bf16[128,1,100]{2,1,0:T(2,128)(2,1)}, u32[]{:S(2)}) copy-start(bf16[128,1,100]{2,1,0:T(2,128)(2,1)} %get-tuple-element.113) | copy-start | bytes 76804
  90.4 27.9 %copy-start.96 = (bf16[128,1,100]{2,1,0:T(2,128)(2,1)S(1)}, bf16[128,1,100]{2,1,0:T(2,128)(2,1)}, u32[]{:S(2)}) copy-start(bf16[128,1,100]{2,1,0:T(2,128)(2,1)} %get-tuple-element.114) | copy-start | bytes 76804
  90.4 29.3 %copy-start.100 = (bf16[128,1,100]{2,1,0:T(2,128)(2,1)S(1)}, bf16[128,1,100]{2,1,0:T(2,128)(2,1)}, u32[]{:S(2)}) copy-start(bf16[128,1,100]{2,1,0:T(2,128)(2,1)} %get-tuple-element.91) | copy-start | bytes 76804
  124.6 469.2 %collective-permute-start.4 = (bf16[100,100]{1,0:T(8,128)(2,1)}, bf16[100,100]{1,0:T(8,128)(2,1)}, u32[]{:S(2)}, u32[]{:S(2)}) collective-permute-start(bf16[100,100]{1,0:T(8,128)(2,1)} %divide_convert_fusion.4), channel_id=1, source_target_pairs={{0,8},{8,16},{16,24},{24,0},{1,9},{9,17},{17,25},{25,1},{2,10},{10... | collective-permute-start | bytes 60008 | tf_op jit(solution)/shard_map/ppermute | solution.py:10
  163.9 31.1 %copy-start.93 = (bf16[625,625]{1,0:T(8,128)(2,1)S(1)}, bf16[625,625]{1,0:T(8,128)(2,1)}, u32[]{:S(2)}) copy-start(bf16[625,625]{1,0:T(8,128)(2,1)} %reshape.223) | copy-start | bytes 2343754
  241.7 5.5 copy-start.40
  243.1 262.4 %collective-permute-start.2 = (bf16[100,100]{1,0:T(8,128)(2,1)}, bf16[100,100]{1,0:T(8,128)(2,1)}, u32[]{:S(2)}, u32[]{:S(2)}) collective-permute-start(bf16[100,100]{1,0:T(8,128)(2,1)} %divide_convert_fusion.5), channel_id=1, source_target_pairs={{0,8},{8,16},{16,24},{24,0},{1,9},{9,17},{17,25},{25,1},{2,10},{10... | collective-permute-start | bytes 60008 | tf_op jit(solution)/shard_map/ppermute | solution.py:10
  247.2 1.3 copy-start.39
  248.6 1.3 copy-start.38
  249.9 1.3 copy-start.37
  252.5 1.3 copy-start.35
  253.9 1.3 copy-start.34
  255.2 1.3 copy-start.33
  256.5 1.4 copy-start.32
  260.4 1.3 copy-start.27
  263.1 1.3 copy-start.24
  265.7 1.3 copy-start.21
  267.0 1.3 copy-start.20
  268.3 1.3 copy-start.18
  269.6 1.4 copy-start.17
  274.9 1.4 copy-start.11
  276.2 1.3 copy-start.9
  313.5 1.7 copy-start.7
  313.5 1.7 copy-start.154
  339.4 46.3 %collective-permute-start.5 = (bf16[2500,100]{0,1:T(8,128)(2,1)}, bf16[2500,100]{0,1:T(8,128)(2,1)}, u32[]{:S(2)}, u32[]{:S(2)}) collective-permute-start(bf16[2500,100]{0,1:T(8,128)(2,1)} %convert_bitcast_fusion), channel_id=1, source_target_pairs={{0,8},{8,16},{16,24},{24,0},{1,9},{9,17},{17,25},{25,1},{2,10},{10... | collective-permute-start | bytes 1500008 | tf_op jit(solution)/shard_map/ppermute | solution.py:10
  350.2 31.7 %copy-start.3 = (f32[2500,100]{1,0:T(8,128)S(1)}, f32[2500,100]{1,0:T(8,128)}, u32[]{:S(2)}) copy-start(f32[2500,100]{1,0:T(8,128)} %reshape.232) | copy-start | bytes 3000004
  350.2 151.8 %collective-permute-start.3 = (bf16[100,2500]{1,0:T(8,128)(2,1)}, bf16[100,2500]{1,0:T(8,128)(2,1)}, u32[]{:S(2)}, u32[]{:S(2)}) collective-permute-start(bf16[100,2500]{1,0:T(8,128)(2,1)} %reshape.246), channel_id=1, source_target_pairs={{0,8},{8,16},{16,24},{24,0},{1,9},{9,17},{17,25},{25,1},{2,10},{10... | collective-permute-start | bytes 1500008 | tf_op jit(solution)/shard_map/ppermute | solution.py:10
  385.2 208.5 %collective-permute-start.8 = (bf16[100,100]{1,0:T(8,128)(2,1)}, bf16[100,100]{1,0:T(8,128)(2,1)}, u32[]{:S(2)}, u32[]{:S(2)}) collective-permute-start(bf16[100,100]{1,0:T(8,128)(2,1)} %divide_convert_fusion.2), channel_id=1, source_target_pairs={{0,1},{1,2},{2,3},{3,4},{4,5},{5,6},{6,7},{7,0},{8,9},{9,10},{10,1... | collective-permute-start | bytes 60008 | tf_op jit(solution)/shard_map/ppermute | solution.py:10
  421.5 31.3 %copy-start.92 = (bf16[625,625]{0,1:T(8,128)(2,1)S(1)}, bf16[625,625]{0,1:T(8,128)(2,1)}, u32[]{:S(2)}) copy-start(bf16[625,625]{0,1:T(8,128)(2,1)} %reshape.235) | copy-start | bytes 2343754
  508.2 2.3 copy-start.43
  511.8 2.5 copy-start.42
  515.6 2.3 copy-start.41
  519.2 2.3 copy-start.31
  522.8 2.3 copy-start.28
  526.5 2.3 copy-start.25
  530.1 2.3 copy-start.22
  533.8 2.3 copy-start.19
  537.4 2.3 copy-start.16
  540.9 2.3 copy-start.13
  544.6 2.3 copy-start.10
  548.2 2.7 copy-start.8
  586.4 3.7 copy-start.6
  590.0 10.8 %collective-permute-start.7 = (bf16[100,2500]{1,0:T(8,128)(2,1)S(1)}, bf16[100,2500]{1,0:T(8,128)(2,1)S(1)}, u32[]{:S(2)}, u32[]{:S(2)}) collective-permute-start(bf16[100,2500]{1,0:T(8,128)(2,1)S(1)} %reshape.249), channel_id=1, source_target_pairs={{0,1},{1,2},{2,3},{3,4},{4,5},{5,6},{6,7},{7,0},{8,9},{9,10},{10,1... | collective-permute-start | bytes 1500008 | tf_op jit(solution)/shard_map/ppermute | solution.py:10
  590.1 18.1 %copy-start.1 = (f32[100,100]{1,0:T(8,128)S(1)}, f32[100,100]{1,0:T(8,128)}, u32[]{:S(2)}) copy-start(f32[100,100]{1,0:T(8,128)} %param.26) | copy-start | bytes 120004
  593.7 7.2 %collective-permute-start.6 = (bf16[100,100]{1,0:T(8,128)(2,1)S(1)}, bf16[100,100]{1,0:T(8,128)(2,1)S(1)}, u32[]{:S(2)}, u32[]{:S(2)}) collective-permute-start(bf16[100,100]{1,0:T(8,128)(2,1)S(1)} %divide_convert_fusion.3), channel_id=1, source_target_pairs={{0,1},{1,2},{2,3},{3,4},{4,5},{5,6},{6,7},{7,0},{8,9},{9,10},{10,1... | collective-permute-start | bytes 60008 | tf_op jit(solution)/shard_map/ppermute | solution.py:10
  (103 other events, 119.1 us)
where the time goes:
time: 619 us; the launch traced here: 608 us
  local copies, waits for them, and re-layouts  359 us (58%)
  matrix products  182 us (29%)
  other arithmetic  43 us (7%)
  starting transfers between devices  9.97 us (2%)
  waiting for transfers between devices  7.1 us (1%)
  between operations  6.93 us (1%)
    squeeze x50, local copies, waits for them, and re-layouts, absorb(): pushed[index]  77.6 us
    dot_general x50, matrix products, absorb(): lax.dot_general(block_in, edge_three[:, index, :], (((0,), (0,)), ((), ()...  67.2 us
    slice x54, local copies, waits for them, and re-layouts, absorb(): block_out[:, index, :]  66.9 us
    convert_element_type x2, local copies, waits for them, and re-layouts, absorb(): jnp.stack(pieces).astype(jnp.bfloat16)  62.4 us
    dot_general x2, matrix products, absorb(): lax.dot_general(arranged, mixed_rows, (((0,), (0,)), ((), ())), preferred...  49.2 us
    slice x4, local copies, waits for them, and re-layouts, absorb(): pushed[index]  44.4 us
    unnamed x328, local copies, waits for them, and re-layouts  36.1 us
    dot_general x50, matrix products, absorb(): jnp.dot(pushed[index], block_out[:, index, :], preferred_element_type=jnp...  34.2 us
  transfers between devices with their start and end apart: 9, of which 1 were waited for; matrix products, arithmetic and copies ran while one was open for 85% of the time, Pallas kernels for 0%

commit v1 on v0

v1 whole, which is shorter than its diff:
```python
import functools

import jax
import jax.numpy as jnp
import numpy as np
from jax import lax
from jax.experimental import pallas as pl
from jax.experimental.pallas import tpu as pltpu
from jax.sharding import PartitionSpec as P

LANES = 128
ROWS = 8
SLOT = 32
GROUP = 10
MIB = 1 << 20
F32 = jnp.float32
BF16 = jnp.bfloat16

NN = (((1,), (0,)), ((), ()))
NT = (((1,), (1,)), ((), ()))
TN = (((0,), (0,)), ((), ()))


def product(left, right, dims=NN):
    return lax.dot_general(left, right, dims, preferred_element_type=F32)


def halves(values):
    high = values.astype(BF16)
    return high, (values - high.astype(F32)).astype(BF16)


def product_split(left, right, dims=NN):
    left_high, left_low = halves(left)
    right_high, right_low = halves(right)
    axis_left, axis_right = dims[0][0][0], dims[0][1][0]
    both = jnp.concatenate([left_high, left_low], axis_left)
    twice = jnp.concatenate([right_high, right_high], axis_right)
    return product(both, twice, dims) + product(left_high, right_low, dims)


def index_of(shape, axis):
    return lax.broadcasted_iota(jnp.int32, shape, axis)


def square_of(ref, bond):
    shape = (LANES, LANES)
    keep = (index_of(shape, 0) < bond) & (index_of(shape, 1) < bond)
    return jnp.where(keep, ref[...].astype(F32), 0.0)


def spread(ref, bond, site):
    shape = (LANES, LANES)
    row, lane = index_of(shape, 0), index_of(shape, 1)
    keep = (row < bond) & (lane < bond)
    pieces = []
    for k in range(site):
        tile, offset = divmod(k * bond, LANES)
        piece = ref[:, tile * LANES : (tile + 1) * LANES].astype(F32)
        if offset:
            piece = pltpu.roll(piece, LANES - offset, 1)
        if offset + bond > LANES:
            more = ref[:, (tile + 1) * LANES : (tile + 2) * LANES].astype(F32)
            piece = jnp.where(lane < LANES - offset, piece, pltpu.roll(more, LANES - offset, 1))
        pieces.append(jnp.where(keep, piece, 0.0).astype(BF16))
    return pieces


def gather_dense(tiles, ref, bond):
    lane = index_of((LANES, LANES), 1)
    total = len(tiles) * bond
    for tile in range(-(-total // LANES)):
        begin = tile * LANES
        value = None
        for k in range(begin // bond, min(len(tiles) - 1, (begin + LANES - 1) // bond) + 1):
            shift = k * bond - begin
            piece = pltpu.roll(tiles[k], shift % LANES, 1) if shift % LANES else tiles[k]
            value = piece if value is None else jnp.where(lane >= shift, piece, value)
        ref[:, begin : begin + LANES] = value.astype(ref.dtype)


def inverse_factors(grams, bond):
    count = -(-bond // ROWS) * ROWS
    shape = (count, LANES)
    row, lane = index_of(shape, 0), index_of(shape, 1)
    inside = (row < bond) & (lane < bond)
    eye = jnp.where(row == lane, 1.0, 0.0)
    work = [jnp.where(inside, gram[:count], eye) for gram in grams]
    done = [[] for _ in grams]
    for first in range(0, count, ROWS):
        height = count - first
        row, lane = index_of((height, LANES), 0), index_of((height, LANES), 1)
        block = (lane >= first) & (lane < first + ROWS)
        start = jnp.where(row == lane - first, 1.0, 0.0)
        small_row, small_lane = index_of((ROWS, LANES), 0), index_of((ROWS, LANES), 1)
        columns = []
        for n, matrix in enumerate(work):
            columns.append(
                [
                    jnp.broadcast_to(matrix[:, first + j : first + j + 1], (height, LANES))
                    for j in range(ROWS)
                ]
            )
            work[n] = jnp.where(block, start, matrix)
        pivots = [jnp.ones((ROWS, LANES), F32) for _ in work]
        for j in range(ROWS):
            for n in range(len(work)):
                column = columns[n]
                pivot = column[j][j : j + 1, :]
                factor = jnp.where(row > j, column[j] * (1.0 / pivot), 0.0)
                work[n] = work[n] - factor * work[n][j : j + 1, :]
                for later in range(j + 1, ROWS):
                    column[later] = column[later] - factor * column[later][j : j + 1, :]
                pivots[n] = jnp.where(small_row == j, pivot, pivots[n])
        for n in range(len(work)):
            scaled = work[n][:ROWS] * lax.rsqrt(pivots[n])
            done[n].append(jnp.where(small_lane <= small_row + first, scaled, 0.0))
            work[n] = work[n][ROWS:]
    tail = jnp.zeros((LANES - count, LANES), F32)
    keep = (index_of((LANES, LANES), 0) < bond) & (index_of((LANES, LANES), 1) < bond)
    return [jnp.where(keep, jnp.concatenate(parts + [tail], 0), 0.0) for parts in done]


def gram_of(values):
    high, low = halves(values)
    both = product(high, jnp.concatenate([high, low], 1), TN)
    mixed = both[:, LANES:]
    return both[:, :LANES] + mixed + mixed.T


def scaled_corner(values, bond):
    mean = jnp.sum(values * values) / (bond * bond)
    return (values / jnp.sqrt(mean + 1e-06)).astype(BF16)


def fill_half(corner, pieces, half_ref):
    for k, piece in enumerate(pieces):
        half_ref[k * LANES : (k + 1) * LANES, :] = product(corner, piece)


def store_frame_rows(inverse, sketched_ref, rows_ref, spare_ref, plain, moved, site):
    plain[...] = jnp.zeros_like(plain)
    moved[...] = jnp.zeros_like(moved)
    bond_rows = plain.shape[0] // SLOT
    for k in range(site):
        tile = product_split(inverse, sketched_ref[k * LANES : (k + 1) * LANES, :], NT)
        place = ROWS * (k // (ROWS - 1)) + 1 + k % (ROWS - 1)
        plain[pl.ds(k, bond_rows, stride=SLOT), :] = tile[:bond_rows]
        moved[pl.ds(place, bond_rows, stride=SLOT), :] = tile[:bond_rows]
    rows_ref[...] = plain[...].astype(BF16)
    spare_ref[...] = moved[...].astype(BF16)


def prepare_kernel(
    bond, site, c1, t1, c4, t3, c2, t2, t4, above, below, right,
    t1_wide, t4_wide, upper, upper_sketch, lower, lower_sketch, side, side_sketch, half,
):
    for k, piece in enumerate(spread(t4, bond, site)):
        t4_wide[:, k * LANES : (k + 1) * LANES] = piece
    first = spread(t1, bond, site)
    for k, piece in enumerate(first):
        t1_wide[:, k * LANES : (k + 1) * LANES] = piece
    jobs = (
        (c1, first, above, upper, upper_sketch),
        (c4, None, below, lower, lower_sketch),
        (c2, None, right, side, side_sketch),
    )
    edges = (None, t3, t2)
    for (corner, pieces, sketch, plain, sketched), edge in zip(jobs, edges):
        pieces = spread(edge, bond, site) if pieces is None else pieces
        fill_half(square_of(corner, bond).astype(BF16), pieces, half)
        plain[...] = half[...].astype(BF16)
        sketched[...] = product_split(half[...], square_of(sketch, bond))


def side_kernel(bond, site, c2, t2, right, side_sketch, half):
    fill_half(square_of(c2, bond).astype(BF16), spread(t2, bond, site), half)
    side_sketch[...] = product_split(half[...], square_of(right, bond))


def vertical_kernel(
    bond, site, c1, t1, c4, t3, above, below, upper, upper_sketch, lower, lower_sketch,
    rows_ref, spare_ref, frame_out, corner_top, corner_bottom, half, over, under, plain, moved,
):
    fill_half(square_of(c1, bond).astype(BF16), spread(t1, bond, site), half)
    under[...] = lower_sketch[...] + product_split(half[...], square_of(above, bond))
    fill_half(square_of(c4, bond).astype(BF16), spread(t3, bond, site), half)
    over[...] = upper_sketch[...] + product_split(half[...], square_of(below, bond))
    grams = [gram_of(over[...]), gram_of(under[...])]
    inverse_over, inverse_under = inverse_factors(grams, bond)
    store_frame_rows(inverse_over, over, rows_ref, spare_ref, plain, moved, site)
    frame_out[...] = product_split(under[...], inverse_under, NT).astype(BF16)
    bond_rows = plain.shape[0] // SLOT
    total = jnp.zeros((bond_rows, LANES), F32)
    for k in range(site):
        piece = plain[pl.ds(k, bond_rows, stride=SLOT), :].astype(BF16)
        total = total + product(piece, upper[k * LANES : (k + 1) * LANES, :])
    corner_top[...] = scaled_corner(total, bond)[:bond, :bond]
    bottom = product(frame_out[...], lower[...], TN)
    corner_bottom[...] = scaled_corner(bottom, bond)[:bond, :bond]


def horizontal_kernel(
    bond, site, c1, edge, left, side, side_sketch,
    inverse_ref, frame_out, corner_left, corner_right, half, total,
):
    corner = square_of(c1, bond).T.astype(BF16)
    for k in range(site):
        half[k * LANES : (k + 1) * LANES, :] = product(corner, edge[:, k * LANES : (k + 1) * LANES])
    total[...] = side_sketch[...] + product_split(half[...], square_of(left, bond))
    (inverse,) = inverse_factors([gram_of(total[...])], bond)
    inverse_ref[...] = inverse
    frame_out[...] = product_split(total[...], inverse, NT).astype(BF16)
    head = product(half[...].astype(BF16), frame_out[...], TN)
    corner_left[...] = scaled_corner(head, bond)[:bond, :bond]
    tail = product(frame_out[...], side[...], TN)
    corner_right[...] = scaled_corner(tail, bond)[:bond, :bond]


def arrive_kernel(
    bond, site, c1, t4, left, side_sketch, inverse_ref, rows_ref, spare_ref, half, total, plain, moved
):
    corner = square_of(c1, bond).T.astype(BF16)
    fill_half(corner, spread(t4, bond, site), half)
    total[...] = side_sketch[...] + product_split(half[...], square_of(left, bond))
    store_frame_rows(inverse_ref[...], total, rows_ref, spare_ref, plain, moved, site)


def absorb_kernel(
    bond, site, rows_ref, spare_ref, edge, tensor, frame_out,
    dense, wide, mixed, pushed, last, result,
):
    main = site - 1
    last[...] = jnp.zeros_like(last)
    result[bond * main :, :] = jnp.zeros((result.shape[0] - bond * main, LANES), F32)

    def step(group, carry):
        begin = pl.multiple_of(group * (GROUP * SLOT), GROUP * SLOT)
        frame = rows_ref[pl.ds(begin, GROUP * SLOT), :]
        spare = product(
            spare_ref[pl.ds(begin, GROUP * SLOT), :], edge[:, main * LANES : site * LANES]
        )
        for pair in range(main // 2):
            both = product(frame, edge[:, 2 * pair * LANES : (2 * pair + 2) * LANES])
            for side in range(2):
                j = 2 * pair + side
                for p in range(GROUP):
                    tile = both[p * SLOT : (p + 1) * SLOT, side * LANES : (side + 1) * LANES]
                    if j * (ROWS - 1) < site:
                        extra = spare[p * SLOT + j * ROWS : p * SLOT + (j + 1) * ROWS, :]
                        tile = jnp.concatenate([tile[: SLOT - ROWS], tile[SLOT - ROWS :] + extra], 0)
                    mixed[j * SLOT : (j + 1) * SLOT, p * LANES : (p + 1) * LANES] = tile.astype(BF16)
        for pair in range(GROUP // 2):
            out = product(tensor[...], mixed[:, 2 * pair * LANES : (2 * pair + 2) * LANES])
            for k in range(site):
                parts = [
                    out[k * main : (k + 1) * main, side * LANES : (side + 1) * LANES]
                    for side in range(2)
                ]
                pushed[2 * pair * main : (2 * pair + 2) * main, k * LANES : (k + 1) * LANES] = (
                    jnp.concatenate(parts, 0).astype(BF16)
                )
            for side in range(2):
                place = group * GROUP + 2 * pair + side
                last[pl.ds(place, site, stride=LANES), :] = out[
                    site * main : site * main + site, side * LANES : (side + 1) * LANES
                ]
        place = pl.multiple_of(group * (GROUP * main), GROUP * main)
        result[pl.ds(place, GROUP * main), :] = product(pushed[...], frame_out[...])
        return carry

    lax.fori_loop(0, bond // GROUP, step, 0)
    tiles = [result[pl.ds(k, LANES, stride=main), :] for k in range(main)]
    joined = jnp.concatenate(
        [last[k * LANES : (k + 1) * LANES, :].astype(BF16) for k in range(site)], 1
    )
    tiles.append(product(joined, frame_out[...]))
    squares = tiles[0] * tiles[0]
    for tile in tiles[1:]:
        squares = squares + tile * tile
    scale = 1.0 / jnp.sqrt(jnp.sum(squares) / (bond * bond * site) + 1e-06)
    tiles = [tile * scale for tile in tiles]
    for k, tile in enumerate(tiles):
        wide[:, k * LANES : (k + 1) * LANES] = tile.astype(BF16)
    gather_dense(tiles, dense, bond)


def arrange_kernel(pattern, tensor, rows_left, columns_left, rows_top, columns_top, left, top):
    square = tensor.shape[0]
    for rows, columns, out in ((rows_left, columns_left, left), (rows_top, columns_top, top)):
        pick_rows = jnp.where(index_of((rows.shape[0], square), 1) == rows[...], 1.0, 0.0)
        pick_columns = jnp.where(index_of((square, columns.shape[1]), 0) == columns[...], 1.0, 0.0)
        turned = product(pick_rows.astype(BF16), tensor[...], NT).astype(BF16)
        out[...] = product(turned, pick_columns.astype(BF16)).astype(BF16)


def places(site):
    main = site - 1
    height = -(-site * site // 16) * 16
    rows = np.full((2, height), -1, np.int32)
    columns = np.full((2, main * SLOT), -1, np.int32)
    for summed in range(site):
        for kept in range(site):
            at = summed * main + kept if kept < main else site * main + summed
            rows[0, at] = summed * site + kept
            rows[1, at] = kept * site + summed
    for edge in range(site):
        for frame in range(site):
            if edge < main:
                at = edge * SLOT + frame
            else:
                slot, offset = divmod(frame, ROWS - 1)
                at = slot * SLOT + SLOT - ROWS + 1 + offset
            columns[0, at] = frame * site + edge
            columns[1, at] = edge * site + frame
    return rows, columns


def call(kernel, args, outs, scratch, limit, blocks=None):
    specs = []
    for arg in args:
        if len(arg.shape) == 2 and (arg.shape[0] % 16 or arg.shape[1] % LANES):
            shape = tuple(-(-size // LANES) * LANES for size in arg.shape)
            specs.append(pl.BlockSpec(shape, lambda i: (0, 0)))
        else:
            specs.append(pl.BlockSpec(arg.shape, lambda i: (0, 0)))
    out_specs = []
    for n, out in enumerate(outs):
        block = out.shape if blocks is None or blocks[n] is None else blocks[n]
        out_specs.append(pl.BlockSpec(block, lambda i: (0, 0)))
    return pl.pallas_call(
        kernel,
        grid=(1,),
        in_specs=specs,
        out_specs=out_specs,
        out_shape=outs,
        scratch_shapes=scratch,
        compiler_params=pltpu.CompilerParams(vmem_limit_bytes=limit * MIB),
    )(*args)


def shape_of(shape, dtype=BF16):
    return jax.ShapeDtypeStruct(shape, dtype)


def shift(value, axis, steps):
    count = lax.axis_size(axis)
    pairs = [(source, (source + steps) % count) for source in range(count)]
    return lax.ppermute(value, axis, pairs)


def shift_both(value, steps_col, steps_row):
    columns, rows = lax.axis_size("col"), lax.axis_size("row")
    pairs = []
    for x in range(columns):
        for y in range(rows):
            target = (x + steps_col) % columns * rows + (y + steps_row) % rows
            pairs.append((x * rows + y, target))
    return lax.ppermute(value, ("col", "row"), pairs)


def body(c1, c2, c4, t1, t2, t3, t4, tensors, pattern, below, above, right, left):
    bond = c1.shape[0]
    site = t1.shape[1] // bond
    square = site * site
    tall = site * LANES
    bond_rows = -(-bond // ROWS) * ROWS
    rows_shape = (bond_rows * SLOT, LANES)
    padded = -(-site * bond // LANES) * LANES

    t1_up, c1_up = shift(t1, "row", -1), shift(c1, "row", -1)
    t3_down, c4_down = shift(t3, "row", 1), shift(c4, "row", 1)
    t2_back, c2_back = shift(t2, "col", 1), shift(c2, "col", 1)

    rows, columns = places(site)
    height, depth = rows.shape[1], columns.shape[1]
    full = lambda shape: pl.BlockSpec(shape, lambda i, pattern: (0, 0))
    tensor_left, tensor_top = pl.pallas_call(
        arrange_kernel,
        grid_spec=pltpu.PrefetchScalarGridSpec(
            num_scalar_prefetch=1,
            grid=(1,),
            in_specs=[
                pl.BlockSpec((None, square, square), lambda i, pattern: (pattern[0], 0, 0)),
                full((height, 1)),
                full((1, depth)),
                full((height, 1)),
                full((1, depth)),
            ],
            out_specs=[full((height, depth)), full((height, depth))],
        ),
        out_shape=[shape_of((height, depth)), shape_of((height, depth))],
        compiler_params=pltpu.CompilerParams(vmem_limit_bytes=24 * MIB),
    )(
        pattern.reshape(1),
        tensors,
        rows[0].reshape(height, 1),
        columns[0].reshape(1, depth),
        rows[1].reshape(height, 1),
        columns[1].reshape(1, depth),
    )

    wide = shape_of((LANES, tall))
    stack = shape_of((tall, LANES))
    stack_f32 = shape_of((tall, LANES), F32)
    half = pltpu.VMEM((tall, LANES), F32)
    frame_scratch = pltpu.VMEM(rows_shape, F32)
    corner = shape_of((bond, bond))

    (t1_wide, t4_wide, upper, upper_sketch, lower, lower_sketch, side, side_sketch) = call(
        functools.partial(prepare_kernel, bond, site),
        (c1, t1, c4, t3, c2, t2, t4, above, below, right),
        [wide, wide, stack, stack_f32, stack, stack_f32, stack, stack_f32],
        [half],
        40,
    )
    rows_left, spare_left, frame_below, corner_top, corner_bottom = call(
        functools.partial(vertical_kernel, bond, site),
        (c1_up, t1_up, c4_down, t3_down, above, below, upper, upper_sketch, lower, lower_sketch),
        [shape_of(rows_shape), shape_of(rows_shape), stack, corner, corner],
        [half, half, half, frame_scratch, frame_scratch],
        40,
    )

    def absorb(rows_in, spare_in, edge, tensor, frame_out):
        main = site - 1
        return call(
            functools.partial(absorb_kernel, bond, site),
            (rows_in, spare_in, edge, tensor, frame_out),
            [shape_of((bond, site * bond)), wide],
            [
                pltpu.VMEM((main * SLOT, GROUP * LANES), BF16),
                pltpu.VMEM((GROUP * main, tall), BF16),
                pltpu.VMEM((tall, LANES), F32),
                pltpu.VMEM((LANES * main, LANES), F32),
            ],
            48,
            [(LANES, padded), None],
        )

    edge_new, edge_wide = absorb(rows_left, spare_left, t4_wide, tensor_left, frame_below)
    left_corner = shift(corner_top, "col", 1)
    left_bottom = shift(corner_bottom, "col", 1)
    left_edge = shift(edge_new, "col", 1)

    inverse, frame_right, corner_left, corner_right = call(
        functools.partial(horizontal_kernel, bond, site),
        (corner_top, edge_wide, left, side, side_sketch),
        [shape_of((LANES, LANES), F32), stack, corner, corner],
        [half, half],
        32,
    )
    inverse_back = shift(inverse, "col", 1)
    top_left = shift_both(corner_left, 1, 1)
    top_right = shift(corner_right, "row", 1)
    (side_back,) = call(
        functools.partial(side_kernel, bond, site), (c2_back, t2_back, right), [stack_f32], [half], 32
    )
    rows_top, spare_top = call(
        functools.partial(arrive_kernel, bond, site),
        (left_corner, left_edge, left, side_back, inverse_back),
        [shape_of(rows_shape), shape_of(rows_shape)],
        [half, half, frame_scratch, frame_scratch],
        40,
    )
    top_new, _ = absorb(rows_top, spare_top, t1_wide, tensor_top, frame_right)
    top_edge = shift(top_new, "row", 1)
    return (left_corner, left_edge, left_bottom, top_left, top_edge, top_right)


def solution(mesh):
    block, whole = P("col", "row"), P()
    in_specs = (block,) * 7 + (whole, block) + (whole,) * 4
    return jax.shard_map(
        body, mesh=mesh, in_specs=in_specs, out_specs=(block,) * 6, check_vma=False
    )
```

time: 619 us -> 130 us (0.21); the launches traced: 608 us -> 129 us
  local copies, waits for them, and re-layouts: 359 us -> 7.74 us
  matrix products: 182 us -> 0 us
  Pallas kernels: 0 us -> 91.2 us
  other arithmetic: 43 us -> 0 us
  starting transfers between devices: 9.97 us -> 17.9 us
    dot_general x117 -> x0, matrix products: 178 us -> none  [the longest x50 67.2 us: absorb(): lax.dot_general(block_in, edge_three[:, index, :], (((0,), (0,)), ((), ()...]
    slice x58 -> x0, local copies, waits for them, and re-layouts: 111 us -> none  [the longest x54 66.9 us: absorb(): block_out[:, index, :]]
    pallas_call x0 -> x8, Pallas kernels: none -> 91.2 us  [the longest x7 87.7 us: call(): pl.pallas_call(kernel, grid=(1,), in_specs=specs, out_specs=out_specs, ou...]
    squeeze x50 -> x0, local copies, waits for them, and re-layouts: 77.6 us -> none  [absorb(): pushed[index]]
    convert_element_type x8 -> x0, local copies, waits for them, and re-layouts: 74.2 us -> none  [the longest x2 62.4 us: absorb(): jnp.stack(pieces).astype(jnp.bfloat16)]
    another operation x10 -> x0, other arithmetic: 36.3 us -> none  [the longest x6 19.6 us: orthonormal(): factor = jnp.linalg.cholesky(gram_matrix)]
    reshape x20 -> x0, local copies, waits for them, and re-layouts: 34.5 us -> none  [the longest x4 9.74 us: corner_edge(): edge_field.reshape(bond_dim, site_dim, bond_dim)]
    unnamed x328 -> x37, local copies, waits for them, and re-layouts: 36.1 us -> 7.74 us
  transfers between devices with their start and end apart: 9 -> 13, of which waited for: 1 -> 2; matrix products, arithmetic and copies ran while one was open for 85% -> 3% of each run, Pallas kernels for 0% -> 44%
where the time goes in v1:
time: 130 us; the launch traced here: 129 us
  Pallas kernels  91.2 us (70%)
  starting transfers between devices  17.9 us (14%)
  waiting for transfers between devices  10.7 us (8%)
  local copies, waits for them, and re-layouts  7.74 us (6%)
  between operations  1.69 us (1%)
    pallas_call x7, Pallas kernels, call(): pl.pallas_call(kernel, grid=(1,), in_specs=specs, out_specs=out_specs, ou...  87.7 us
    ppermute x12, starting transfers between devices, shift(): return lax.ppermute(value, axis, pairs)  17.6 us
    ppermute x1, waiting for transfers between devices, shift_both(): return lax.ppermute(value, ('col', 'row'), pairs)  7.89 us
    unnamed x37, local copies, waits for them, and re-layouts  7.74 us
    pallas_call x1, Pallas kernels, body(): pl.pallas_call(arrange_kernel, grid_spec=pltpu.PrefetchScalarGridSpec(num...  3.49 us
    ppermute x12, waiting for transfers between devices, shift(): return lax.ppermute(value, axis, pairs)  2.85 us
  transfers between devices with their start and end apart: 13, of which 2 were waited for; matrix products, arithmetic and copies ran while one was open for 3% of the time, Pallas kernels for 44%

profile of v1, /device:TPU:0, one launch (start us, length us, event | category | flops | bytes accessed | tf_op | source)
XLA Modules:
  0.0 129.3 jit_solution(2219004416906322253)
XLA Ops:
  0.6 0.0 copy-start.1
  0.6 0.0 copy-start.2
  0.7 0.0 copy-start.10
  0.7 0.0 copy-start.11
  0.7 0.0 copy-start.3
  0.7 0.0 copy-start.12
  0.7 0.0 copy-start
  0.7 0.0 copy-start.8
  0.7 0.0 copy-start.7
  0.7 0.0 copy-start.6
  0.7 4.5 %collective-permute-start.1 = (bf16[100,2500]{1,0:T(8,128)(2,1)}, bf16[100,2500]{1,0:T(8,128)(2,1)}, u32[]{:S(2)}, u32[]{:S(2)}) collective-permute-start(bf16[100,2500]{1,0:T(8,128)(2,1)} %t1.1), channel_id=1, source_target_pairs={{0,7},{1,0},{2,1},{3,2},{4,3},{5,4},{6,5},{7,6},{8,15},{9,8},{10,9... | collective-permute-start | bytes 1500008 | tf_op jit(solution)/shard_map/ppermute | solution.py:349
  5.3 0.0 collective-permute-start.3
  5.3 3.5 %collective-permute-start = (bf16[100,100]{1,0:T(8,128)(2,1)}, bf16[100,100]{1,0:T(8,128)(2,1)S(1)}, u32[]{:S(2)}, u32[]{:S(2)}) collective-permute-start(bf16[100,100]{1,0:T(8,128)(2,1)} %c1.1), channel_id=1, source_target_pairs={{0,7},{1,0},{2,1},{3,2},{4,3},{5,4},{6,5},{7,6},{8,15},{9,8},{10,9... | collective-permute-start | bytes 60008 | tf_op jit(solution)/shard_map/ppermute | solution.py:349
  8.8 0.0 collective-permute-start.2
  8.8 1.5 %collective-permute-start.9 = (bf16[100,2500]{1,0:T(8,128)(2,1)}, bf16[100,2500]{1,0:T(8,128)(2,1)}, u32[]{:S(2)}, u32[]{:S(2)}) collective-permute-start(bf16[100,2500]{1,0:T(8,128)(2,1)} %t2.1), channel_id=1, source_target_pairs={{0,8},{8,16},{16,24},{24,0},{1,9},{9,17},{17,25},{25,1},{2,10},{10... | collective-permute-start | bytes 1500008 | tf_op jit(solution)/shard_map/ppermute | solution.py:349
  10.3 3.6 %copy.23.tensor = bf16[8,625,625]{2,1,0:T(8,128)(2,1)S(1)} copy(bf16[8,625,625]{2,0,1:T(8,128)(2,1)} %param.24) | data formatting | bytes 12500000 | tf_op args[7]
  14.0 0.0 copy-start.4
  14.0 0.0 copy-start.5
  14.0 0.0 copy-start.13
  14.0 0.0 copy-start.14
  14.7 0.0 copy-done.1
  14.7 0.0 copy-done.2
  14.7 0.0 copy-done.10
  14.7 0.0 copy-done.11
  14.8 0.0 copy-done.3
  14.8 0.0 copy-done.12
  14.8 0.0 copy-done
  14.8 0.0 copy-done.8
  14.8 3.1 %shard_map.208 = (bf16[128,3200]{1,0:T(8,128)(2,1)S(1)}, bf16[128,3200]{1,0:T(8,128)(2,1)S(1)}, bf16[3200,128]{1,0:T(8,128)(2,1)S(1)}, f32[3200,128]{1,0:T(8,128...) custom-call(bf16[100,100]{1,0:T(8,128)(2,1)S(1)} %copy-done.10, ...), custom_call_target="tpu_custom_call" | custom-call | tf_op jit(solution)/shard_map/pallas_call | solution.py:331
  17.9 3.5 %shard_map.210 = (bf16[640,768]{1,0:T(8,128)(2,1)S(1)}, bf16[640,768]{1,0:T(8,128)(2,1)S(1)}) custom-call(s32[1]{0:T(128)} %bitcast.1.pattern, bf16[8,625,625]{2,1,0:T(8,128)(2,1)S(1)} %copy.23.tensor, s32[640,1]{1,0:T(8,128)S(1)} %copy-done.5, s32[1,768]{1,0:T(1,128)S(1)} %copy-done.14, s32[640,1]{1,0:T(8,128)S(1)} %copy-done.4, s32[1,768]{1,0:T(1,128)S(1)} %copy-done.13), custom_call_target="tpu_custom_call" | custom-call | tf_op jit(solution)/shard_map/pallas_call | solution.py:378
  21.4 0.0 collective-permute-done.c1
  21.4 0.0 collective-permute-done.2.c4
  21.4 0.0 collective-permute-done.1.t1
  21.4 0.0 collective-permute-done.3.t3
  21.4 12.7 %shard_map.209 = (bf16[3328,128]{1,0:T(8,128)(2,1)S(1)}, bf16[3328,128]{1,0:T(8,128)(2,1)S(1)}, bf16[3200,128]{1,0:T(8,128)(2,1)S(1)}, bf16[100,100]{1,0:T(8,128)(2,1)S(1)}, bf16[100,100]{1,0:T(8,128)(2,1)S(1)}) custom-call(bf16[100,100]{1,0:T(8,128)(2,1)S(1)} %collective-permute-done.c1, bf16[100,2500]{1,0:T(8,128)(2,1)} %collective-permute-done.1.t1, ...), custom_call_target="tpu_custom_call" | custom-call | tf_op jit(solution)/shard_map/pallas_call | solution.py:331
  34.2 0.0 copy-start.9
  34.2 29.4 %shard_map.211 = (bf16[100,2500]{1,0:T(8,128)(2,1)S(1)}, bf16[128,3200]{1,0:T(8,128)(2,1)S(1)}) custom-call(bf16[3328,128]{1,0:T(8,128)(2,1)S(1)} %get-tuple-element.35.rows_ref, bf16[3328,128]{1,0:T(8,128)(2,1)S(1)} %get-tuple-element.36.spare_ref, bf16[128,3200]{1,0:T(8,128)(2,1)S(1)} %get-tuple-element.37.edge, ...), custom_call_target="tpu_custom_call" | custom-call | tf_op jit(solution)/shard_map/pallas_call | solution.py:331
  63.6 1.5 %collective-permute-start.5 = (bf16[100,2500]{1,0:T(8,128)(2,1)S(1)}, bf16[100,2500]{1,0:T(8,128)(2,1)S(1)}, u32[]{:S(2)}, u32[]{:S(2)}) collective-permute-start(bf16[100,2500]{1,0:T(8,128)(2,1)S(1)} %get-tuple-element.40), channel_id=1, source_target_pairs={{0,8},{8,16},{16,24},{24,0},{1,9},{9,17},{17,25},{25,1},{2,10},{10... | collective-permute-start | bytes 1500008 | tf_op jit(solution)/shard_map/ppermute | solution.py:349
  65.1 6.4 %shard_map.212 = (f32[128,128]{1,0:T(8,128)S(1)}, bf16[3200,128]{1,0:T(8,128)(2,1)S(1)}, bf16[100,100]{1,0:T(8,128)(2,1)S(1)}, bf16[100,100]{1,0:T(8,128)(2,1)S(1)}) custom-call(bf16[100,100]{1,0:T(8,128)(2,1)S(1)} %get-tuple-element.34.c1, bf16[128,3200]{1,0:T(8,128)(2,1)S(1)} %get-tuple-element.42.edge, f32[100,100]{1,0:T(8,128)S(1)} %copy-done.9, ...), custom_call_target="tpu_custom_call" | custom-call | tf_op jit(solution)/shard_map/pallas_call | solution.py:331
  71.6 1.5 %collective-permute-start.10 = (f32[128,128]{1,0:T(8,128)S(1)}, f32[128,128]{1,0:T(8,128)S(1)}, u32[]{:S(2)}, u32[]{:S(2)}) collective-permute-start(f32[128,128]{1,0:T(8,128)S(1)} %get-tuple-element.46), channel_id=1, source_target_pairs={{0,8},{8,16},{16,24},{24,0},{1,9},{9,17},{17,25},{25,1},{2,10},{10... | collective-permute-start | bytes 196616 | tf_op jit(solution)/shard_map/ppermute | solution.py:349
  73.1 0.5 collective-permute-start.8
  73.6 1.5 %collective-permute-start.4 = (bf16[100,100]{1,0:T(8,128)(2,1)S(1)}, bf16[100,100]{1,0:T(8,128)(2,1)S(1)}, u32[]{:S(2)}, u32[]{:S(2)}) collective-permute-start(bf16[100,100]{1,0:T(8,128)(2,1)S(1)} %get-tuple-element.34.c1), channel_id=1, source_target_pairs={{0,8},{8,16},{16,24},{24,0},{1,9},{9,17},{17,25},{25,1},{2,10},{10... | collective-permute-start | bytes 60008 | tf_op jit(solution)/shard_map/ppermute | solution.py:349
  75.1 2.8 %collective-permute-done.8.c2 = bf16[100,100]{1,0:T(8,128)(2,1)S(1)} collective-permute-done((bf16[100,100]{1,0:T(8,128)(2,1)S(1)}, bf16[100,100]{1,0:T(8,128)(2,1)S(1)}, u32[]{:S(2)}, u32[]{:S(2)}) %collective-permute-start.8) | collective-permute-done | bytes 20032 | tf_op jit(solution)/shard_map/ppermute | solution.py:349
  77.9 0.0 collective-permute-done.9.t2
  77.9 2.2 %shard_map.213.side_sketch = f32[3200,128]{1,0:T(8,128)S(1)} custom-call(bf16[100,100]{1,0:T(8,128)(2,1)S(1)} %collective-permute-done.8.c2, bf16[100,2500]{1,0:T(8,128)(2,1)} %collective-permute-done.9.t2, f32[100,100]{1,0:T(8,128)S(1)} %copy-done.6), custom_call_target="tpu_custom_call" | custom-call | tf_op jit(solution)/shard_map/pallas_call | solution.py:331
  80.1 0.0 collective-permute-done.4.c1
  80.1 0.0 collective-permute-done.10.inverse_ref
  80.1 0.0 collective-permute-done.5.t4
  80.1 3.8 %shard_map.214 = (bf16[3328,128]{1,0:T(8,128)(2,1)S(1)}, bf16[3328,128]{1,0:T(8,128)(2,1)S(1)}) custom-call(bf16[100,100]{1,0:T(8,128)(2,1)S(1)} %collective-permute-done.4.c1, bf16[100,2500]{1,0:T(8,128)(2,1)S(1)} %collective-permute-done.5.t4, f32[100,100]{1,0:T(8,128)S(1)} %copy-done.9, f32[3200,128]{1,0:T(8,128)S(1)} %shard_map.213.side_sketch, ...), custom_call_target="tpu_custom_call" | custom-call | tf_op jit(solution)/shard_map/pallas_call | solution.py:331
  83.9 30.2 %shard_map.215 = (bf16[100,2500]{1,0:T(8,128)(2,1)S(1)}, bf16[128,3200]{1,0:T(8,128)(2,1)}) custom-call(bf16[3328,128]{1,0:T(8,128)(2,1)S(1)} %get-tuple-element.47.rows_ref, bf16[3328,128]{1,0:T(8,128)(2,1)S(1)} %get-tuple-element.48.spare_ref, bf16[128,3200]{1,0:T(8,128)(2,1)S(1)} %get-tuple-element.49.edge, ...), custom_call_target="tpu_custom_call" | custom-call | tf_op jit(solution)/shard_map/pallas_call | solution.py:331
  114.1 0.0 collective-permute-start.11
  114.1 0.4 collective-permute-start.7
  114.4 0.5 collective-permute-start.12
  114.9 2.4 %collective-permute-start.6 = (bf16[100,100]{1,0:T(8,128)(2,1)S(1)}, bf16[100,100]{1,0:T(8,128)(2,1)S(1)}, u32[]{:S(2)}, u32[]{:S(2)}) collective-permute-start(bf16[100,100]{1,0:T(8,128)(2,1)S(1)} %get-tuple-element.41), channel_id=1, source_target_pairs={{0,8},{8,16},{16,24},{24,0},{1,9},{9,17},{17,25},{25,1},{2,10},{10... | collective-permute-start | bytes 60008 | tf_op jit(solution)/shard_map/ppermute | solution.py:349
  117.3 7.9 %collective-permute-done.7 = bf16[100,100]{1,0:T(8,128)(2,1)S(1)} collective-permute-done((bf16[100,100]{1,0:T(8,128)(2,1)S(1)}, bf16[100,100]{1,0:T(8,128)(2,1)S(1)}, u32[]{:S(2)}, u32[]{:S(2)}) %collective-permute-start.7) | collective-permute-done | bytes 20032 | tf_op jit(solution)/shard_map/ppermute | solution.py:359
  125.2 0.0 collective-permute-done.12
  125.3 0.0 collective-permute-done.6
  125.3 0.0 collective-permute-done.11
  125.3 0.6 copy.31
  125.9 0.8 copy.32
  126.7 0.6 copy.33
  127.3 0.6 copy.34
  127.9 0.8 copy.35
  128.7 0.6 copy.36
  (7 shorter events, 0.0 us)
Async XLA Ops:
  0.6 14.1 %copy-start.1 = (bf16[100,2500]{1,0:T(8,128)(2,1)S(1)}, bf16[100,2500]{1,0:T(8,128)(2,1)}, u32[]{:S(2)}) copy-start(bf16[100,2500]{1,0:T(8,128)(2,1)} %t1.1) | copy-start | bytes 1500004
  0.6 14.1 %copy-start.2 = (bf16[100,2500]{1,0:T(8,128)(2,1)S(1)}, bf16[100,2500]{1,0:T(8,128)(2,1)}, u32[]{:S(2)}) copy-start(bf16[100,2500]{1,0:T(8,128)(2,1)} %t3.1) | copy-start | bytes 1500004
  0.7 14.1 %copy-start.10 = (bf16[100,100]{1,0:T(8,128)(2,1)S(1)}, bf16[100,100]{1,0:T(8,128)(2,1)}, u32[]{:S(2)}) copy-start(bf16[100,100]{1,0:T(8,128)(2,1)} %c1.1) | copy-start | bytes 60004
  0.7 14.1 %copy-start.11 = (bf16[100,100]{1,0:T(8,128)(2,1)S(1)}, bf16[100,100]{1,0:T(8,128)(2,1)}, u32[]{:S(2)}) copy-start(bf16[100,100]{1,0:T(8,128)(2,1)} %c4.1) | copy-start | bytes 60004
  0.7 14.1 %copy-start.3 = (bf16[100,2500]{1,0:T(8,128)(2,1)S(1)}, bf16[100,2500]{1,0:T(8,128)(2,1)}, u32[]{:S(2)}) copy-start(bf16[100,2500]{1,0:T(8,128)(2,1)} %t2.1) | copy-start | bytes 1500004
  0.7 14.1 %copy-start.12 = (bf16[100,100]{1,0:T(8,128)(2,1)S(1)}, bf16[100,100]{1,0:T(8,128)(2,1)}, u32[]{:S(2)}) copy-start(bf16[100,100]{1,0:T(8,128)(2,1)} %c2.1) | copy-start | bytes 60004
  0.7 14.1 %copy-start = (bf16[100,2500]{1,0:T(8,128)(2,1)S(1)}, bf16[100,2500]{1,0:T(8,128)(2,1)}, u32[]{:S(2)}) copy-start(bf16[100,2500]{1,0:T(8,128)(2,1)} %t4.1) | copy-start | bytes 1500004
  0.7 14.1 %copy-start.8 = (f32[100,100]{1,0:T(8,128)S(1)}, f32[100,100]{1,0:T(8,128)}, u32[]{:S(2)}) copy-start(f32[100,100]{1,0:T(8,128)} %below.3) | copy-start | bytes 120004
  0.7 14.1 %copy-start.7 = (f32[100,100]{1,0:T(8,128)S(1)}, f32[100,100]{1,0:T(8,128)}, u32[]{:S(2)}) copy-start(f32[100,100]{1,0:T(8,128)} %above.3) | copy-start | bytes 120004
  0.7 14.1 %copy-start.6 = (f32[100,100]{1,0:T(8,128)S(1)}, f32[100,100]{1,0:T(8,128)}, u32[]{:S(2)}) copy-start(f32[100,100]{1,0:T(8,128)} %right.3) | copy-start | bytes 120004
  0.7 20.7 %collective-permute-start.1 = (bf16[100,2500]{1,0:T(8,128)(2,1)}, bf16[100,2500]{1,0:T(8,128)(2,1)}, u32[]{:S(2)}, u32[]{:S(2)}) collective-permute-start(bf16[100,2500]{1,0:T(8,128)(2,1)} %t1.1), channel_id=1, source_target_pairs={{0,7},{1,0},{2,1},{3,2},{4,3},{5,4},{6,5},{7,6},{8,15},{9,8},{10,9... | collective-permute-start | bytes 1500008 | tf_op jit(solution)/shard_map/ppermute | solution.py:349
  5.3 16.2 %collective-permute-start.3 = (bf16[100,2500]{1,0:T(8,128)(2,1)}, bf16[100,2500]{1,0:T(8,128)(2,1)}, u32[]{:S(2)}, u32[]{:S(2)}) collective-permute-start(bf16[100,2500]{1,0:T(8,128)(2,1)} %t3.1), channel_id=1, source_target_pairs={{0,1},{1,2},{2,3},{3,4},{4,5},{5,6},{6,7},{7,0},{8,9},{9,10},{10,1... | collective-permute-start | bytes 1500008 | tf_op jit(solution)/shard_map/ppermute | solution.py:349
  5.3 16.1 %collective-permute-start = (bf16[100,100]{1,0:T(8,128)(2,1)}, bf16[100,100]{1,0:T(8,128)(2,1)S(1)}, u32[]{:S(2)}, u32[]{:S(2)}) collective-permute-start(bf16[100,100]{1,0:T(8,128)(2,1)} %c1.1), channel_id=1, source_target_pairs={{0,7},{1,0},{2,1},{3,2},{4,3},{5,4},{6,5},{7,6},{8,15},{9,8},{10,9... | collective-permute-start | bytes 60008 | tf_op jit(solution)/shard_map/ppermute | solution.py:349
  8.8 12.6 %collective-permute-start.2 = (bf16[100,100]{1,0:T(8,128)(2,1)}, bf16[100,100]{1,0:T(8,128)(2,1)S(1)}, u32[]{:S(2)}, u32[]{:S(2)}) collective-permute-start(bf16[100,100]{1,0:T(8,128)(2,1)} %c4.1), channel_id=1, source_target_pairs={{0,1},{1,2},{2,3},{3,4},{4,5},{5,6},{6,7},{7,0},{8,9},{9,10},{10,1... | collective-permute-start | bytes 60008 | tf_op jit(solution)/shard_map/ppermute | solution.py:349
  8.8 69.0 %collective-permute-start.9 = (bf16[100,2500]{1,0:T(8,128)(2,1)}, bf16[100,2500]{1,0:T(8,128)(2,1)}, u32[]{:S(2)}, u32[]{:S(2)}) collective-permute-start(bf16[100,2500]{1,0:T(8,128)(2,1)} %t2.1), channel_id=1, source_target_pairs={{0,8},{8,16},{16,24},{24,0},{1,9},{9,17},{17,25},{25,1},{2,10},{10... | collective-permute-start | bytes 1500008 | tf_op jit(solution)/shard_map/ppermute | solution.py:349
  14.0 3.9 %copy-start.4 = (s32[640,1]{1,0:T(8,128)S(1)}, s32[640,1]{1,0:T(8,128)}, u32[]{:S(2)}) copy-start(s32[640,1]{1,0:T(8,128)} %constant.10.clone.rows_top) | copy-start | bytes 7684
  14.0 3.9 %copy-start.5 = (s32[640,1]{1,0:T(8,128)S(1)}, s32[640,1]{1,0:T(8,128)}, u32[]{:S(2)}) copy-start(s32[640,1]{1,0:T(8,128)} %constant.8.clone.rows_left) | copy-start | bytes 7684
  14.0 3.9 %copy-start.13 = (s32[1,768]{1,0:T(1,128)S(1)}, s32[1,768]{1,0:T(1,128)}, u32[]{:S(2)}) copy-start(s32[1,768]{1,0:T(1,128)} %constant.11.clone.columns_top) | copy-start | bytes 9220
  14.0 3.9 %copy-start.14 = (s32[1,768]{1,0:T(1,128)S(1)}, s32[1,768]{1,0:T(1,128)}, u32[]{:S(2)}) copy-start(s32[1,768]{1,0:T(1,128)} %constant.9.clone.columns_left) | copy-start | bytes 9220
  34.2 30.9 %copy-start.9 = (f32[100,100]{1,0:T(8,128)S(1)}, f32[100,100]{1,0:T(8,128)}, u32[]{:S(2)}) copy-start(f32[100,100]{1,0:T(8,128)} %left.3) | copy-start | bytes 120004
  63.6 16.5 %collective-permute-start.5 = (bf16[100,2500]{1,0:T(8,128)(2,1)S(1)}, bf16[100,2500]{1,0:T(8,128)(2,1)S(1)}, u32[]{:S(2)}, u32[]{:S(2)}) collective-permute-start(bf16[100,2500]{1,0:T(8,128)(2,1)S(1)} %get-tuple-element.40), channel_id=1, source_target_pairs={{0,8},{8,16},{16,24},{24,0},{1,9},{9,17},{17,25},{25,1},{2,10},{10... | collective-permute-start | bytes 1500008 | tf_op jit(solution)/shard_map/ppermute | solution.py:349
  71.6 8.5 %collective-permute-start.10 = (f32[128,128]{1,0:T(8,128)S(1)}, f32[128,128]{1,0:T(8,128)S(1)}, u32[]{:S(2)}, u32[]{:S(2)}) collective-permute-start(f32[128,128]{1,0:T(8,128)S(1)} %get-tuple-element.46), channel_id=1, source_target_pairs={{0,8},{8,16},{16,24},{24,0},{1,9},{9,17},{17,25},{25,1},{2,10},{10... | collective-permute-start | bytes 196616 | tf_op jit(solution)/shard_map/ppermute | solution.py:349
  73.1 4.7 %collective-permute-start.8 = (bf16[100,100]{1,0:T(8,128)(2,1)S(1)}, bf16[100,100]{1,0:T(8,128)(2,1)S(1)}, u32[]{:S(2)}, u32[]{:S(2)}) collective-permute-start(bf16[100,100]{1,0:T(8,128)(2,1)S(1)} %copy-done.12), channel_id=1, source_target_pairs={{0,8},{8,16},{16,24},{24,0},{1,9},{9,17},{17,25},{25,1},{2,10},{10... | collective-permute-start | bytes 60008 | tf_op jit(solution)/shard_map/ppermute | solution.py:349
  73.6 6.5 %collective-permute-start.4 = (bf16[100,100]{1,0:T(8,128)(2,1)S(1)}, bf16[100,100]{1,0:T(8,128)(2,1)S(1)}, u32[]{:S(2)}, u32[]{:S(2)}) collective-permute-start(bf16[100,100]{1,0:T(8,128)(2,1)S(1)} %get-tuple-element.34.c1), channel_id=1, source_target_pairs={{0,8},{8,16},{16,24},{24,0},{1,9},{9,17},{17,25},{25,1},{2,10},{10... | collective-permute-start | bytes 60008 | tf_op jit(solution)/shard_map/ppermute | solution.py:349
  114.1 11.2 %collective-permute-start.11 = (bf16[100,2500]{1,0:T(8,128)(2,1)S(1)}, bf16[100,2500]{1,0:T(8,128)(2,1)S(1)}, u32[]{:S(2)}, u32[]{:S(2)}) collective-permute-start(bf16[100,2500]{1,0:T(8,128)(2,1)S(1)} %get-tuple-element.52), channel_id=1, source_target_pairs={{0,1},{1,2},{2,3},{3,4},{4,5},{5,6},{6,7},{7,0},{8,9},{9,10},{10,1... | collective-permute-start | bytes 1500008 | tf_op jit(solution)/shard_map/ppermute | solution.py:349
  114.1 11.2 %collective-permute-start.7 = (bf16[100,100]{1,0:T(8,128)(2,1)S(1)}, bf16[100,100]{1,0:T(8,128)(2,1)S(1)}, u32[]{:S(2)}, u32[]{:S(2)}) collective-permute-start(bf16[100,100]{1,0:T(8,128)(2,1)S(1)} %get-tuple-element.45), channel_id=1, source_target_pairs={{0,9},{1,10},{2,11},{3,12},{4,13},{5,14},{6,15},{7,8},{8,17},{9,18... | collective-permute-start | bytes 60008 | tf_op jit(solution)/shard_map/ppermute | solution.py:359
  114.4 10.9 %collective-permute-start.12 = (bf16[100,100]{1,0:T(8,128)(2,1)S(1)}, bf16[100,100]{1,0:T(8,128)(2,1)S(1)}, u32[]{:S(2)}, u32[]{:S(2)}) collective-permute-start(bf16[100,100]{1,0:T(8,128)(2,1)S(1)} %get-tuple-element.53), channel_id=1, source_target_pairs={{0,1},{1,2},{2,3},{3,4},{4,5},{5,6},{6,7},{7,0},{8,9},{9,10},{10,1... | collective-permute-start | bytes 60008 | tf_op jit(solution)/shard_map/ppermute | solution.py:349
  114.9 10.3 %collective-permute-start.6 = (bf16[100,100]{1,0:T(8,128)(2,1)S(1)}, bf16[100,100]{1,0:T(8,128)(2,1)S(1)}, u32[]{:S(2)}, u32[]{:S(2)}) collective-permute-start(bf16[100,100]{1,0:T(8,128)(2,1)S(1)} %get-tuple-element.41), channel_id=1, source_target_pairs={{0,8},{8,16},{16,24},{24,0},{1,9},{9,17},{17,25},{25,1},{2,10},{10... | collective-permute-start | bytes 60008 | tf_op jit(solution)/shard_map/ppermute | solution.py:349
